TPU v7x, 1024 devices: a whole 4x4x32 slice. The times are simulated.
1024 devices in a mesh: grp: 16 (over x, y), blk: 64 (over z, core).
Axes of the slice: x: 4, y: 4, z: 32, core: 2. Of those that a mesh axis runs over, the one named last changes fastest.
Arguments:
- charges: bfloat16 [64, 131072], P(None, ('grp', 'blk')), may hold values from -6 to 6
- near_blocks: bfloat16 [1024, 7, 128, 128], P(('grp', 'blk')), may hold values from -0.5 to 0.5
- near_offset: int32 [1024, 7], P(('grp', 'blk')), may hold values from -3 to 3, as said below
- near_count: int32 [1024], P(('grp', 'blk')), may hold values from 1 to 7, as said below
- far_group: int32 [1024, 48], P(('grp', 'blk')), may hold values from 0 to 15
- far_target: int32 [1024, 48, 1], P(('grp', 'blk')), may hold values from 0 to 63; in each aligned block of 48 rows (0 to 47, 48 to 95, ..., all dimensions but the last counted through in order) at most 2 rows name the same one
- far_v: bfloat16 [1024, 48, 32, 128], P(('grp', 'blk')), may hold values from -0.5 to 0.5
- far_u: bfloat16 [1024, 48, 32, 128], P(('grp', 'blk')), may hold values from -0.15625 to 0.15625
Outputs:
- potentials: bfloat16 [64, 131072], P(None, ('grp', 'blk'))
Inputs may be any that keep to these rules, and one draw needn't show every extreme that they name: `near_offset`: the offsets of one device are distinct; the first near_count of them lead to a cluster of the same group. `near_count`: in every group some device has 7 live blocks. `far_target`: among the 48 blocks of one device no target is named more than 2 times; some device names one target exactly 2 times.
All inputs are finite; a program needn't handle non-finite values.
Results may differ from a plain program's by a relative error of at most 0.003.
Values may be sent and summed in bfloat16 or wider, within the bound.
No kernel may reach another device: no remote copies, remote signals or barrier semaphores. Data moves between devices by JAX's collectives and lax.ppermute only.
A program may use at most 32 MiB of HBM per device.

v0:
```python
import jax
import jax.numpy as jnp
from jax import lax
from jax.experimental import pallas as pl
from jax.experimental.pallas import tpu as pltpu
from jax.sharding import PartitionSpec as P

VMEM = pltpu.VMEM
SMEM = pltpu.SMEM
REACH = 4


def local_call(kernel, outs, scalars, arrays, flops, name):
    scalars = () if scalars is None else (scalars,)
    return pl.pallas_call(
        kernel,
        out_shape=outs,
        in_specs=[pl.BlockSpec(memory_space=SMEM)] * len(scalars)
        + [pl.BlockSpec(memory_space=VMEM)] * len(arrays),
        out_specs=jax.tree.map(lambda _: pl.BlockSpec(memory_space=VMEM), outs),
        compiler_params=pltpu.CompilerParams(vmem_limit_bytes=24 << 20),
        cost_estimate=pl.CostEstimate(
            flops=flops, bytes_accessed=sum(a.nbytes for a in arrays), transcendentals=0
        ),
        name=name,
    )(*scalars, *arrays)


def times_transposed(a, b):
    return lax.dot_general(a, b, (((1,), (1,)), ((), ())), preferred_element_type=jnp.float32)


def far_slots(target, here, core, chips):
    half = chips // 2
    ahead = lax.bitwise_and(lax.shift_right_logical(target, 1) - here, chips - 1)
    behind = (ahead >= half).astype(jnp.int32)
    steps = lax.bitwise_and(jnp.where(ahead >= half, chips - ahead, ahead), half - 1)
    slot = lax.bitwise_and(steps, REACH - 1) * (half // REACH) + lax.div(steps, REACH)
    slot = slot * 2 + lax.bitwise_and(target, 1)
    return slot + lax.bitwise_xor(behind, core) * chips


def far_kernel(number_ref, pooled_ref, v_ref, u_ref, out_ref, first_ref):
    blocks, last = v_ref.shape[0], out_ref.shape[0] - 1
    for slot in range(last):
        out_ref[slot] = jnp.zeros(out_ref.shape[1:], jnp.float32)
    first_ref[...] = jnp.where(
        number_ref[2 * blocks + 1] == 0,
        jnp.ones(first_ref.shape, jnp.float32),
        jnp.zeros(first_ref.shape, jnp.float32),
    )
    out_ref[last] = pooled_ref[number_ref[2 * blocks]].astype(jnp.float32)
    step = 16
    for base in range(0, blocks, step):
        parts = []
        for k in range(base, base + step):
            coeff = times_transposed(pooled_ref[number_ref[k]], v_ref[k])
            parts.append(
                jnp.dot(coeff.astype(jnp.bfloat16), u_ref[k], preferred_element_type=jnp.float32)
            )
        for k, part in zip(range(base, base + step), parts):
            out_ref[number_ref[blocks + k]] += part


def chip_kernel(first_ref, parts_ref, taken_ref, own_ref, mine_ref, over_ref, *sent_refs):
    size = own_ref.shape[0]
    nearest = parts_ref[:2] + taken_ref[:2]
    own_ref[:2] = jnp.where(first_ref[...] > 0, nearest, jnp.zeros_like(nearest))
    over_ref[...] = nearest.astype(jnp.bfloat16)
    own_ref[2:] = parts_ref[2:size] + taken_ref[2:size]
    for step, sent_ref in enumerate(sent_refs, 1):
        at = pl.ds(step * size, size)
        sent_ref[:size] = (parts_ref[at] + taken_ref[at]).astype(jnp.bfloat16)
    mine = parts_ref[parts_ref.shape[0] - 1].astype(jnp.bfloat16)
    other = taken_ref[taken_ref.shape[0] - 1].astype(jnp.bfloat16)
    pair = jnp.stack([mine, other])
    mine_ref[...] = pair
    sent_refs[0][size:] = pair
    sent_refs[1][size] = other
    sent_refs[2][size:] = pair


def gather_kernel(*refs):
    (opposite_ref, *came_refs), own_ref, keep_ref = refs[:REACH], refs[REACH], refs[REACH + 1]
    sent_refs = refs[REACH + 2 :]
    for hop in range(len(sent_refs) + 1):
        at = pl.ds(2 * hop, 2)
        total = own_ref[at]
        for came_ref in came_refs:
            total = total + came_ref[at].astype(jnp.float32)
        if hop == 0:
            keep_ref[...] = total
            continue
        if hop == len(sent_refs):
            total = total + opposite_ref[...].astype(jnp.float32)
        sent_refs[hop - 1][...] = total.astype(jnp.bfloat16)


def near_kernel(
    number_ref, unused_ref, third_ref, next_ref, mine_ref, blocks_ref, out_ref, far_on_ref
):
    slots = blocks_ref.shape[0]
    last = next_ref.shape[0] - 1
    here = [third_ref[last - 1], next_ref[last - 1], next_ref[last], mine_ref[0], mine_ref[1]]
    total = jnp.zeros(out_ref.shape, jnp.float32)
    far_on = [(jnp.int32(0), jnp.int32(0))] * 2
    for k in range(slots):
        place = number_ref[k]
        source = jnp.zeros_like(here[0])
        for i, cluster in enumerate(here):
            source = jnp.where(place == i, cluster, source)
        total += times_transposed(source, blocks_ref[k])
        for i, (slot, found) in enumerate(far_on):
            hit = place == slots - 1 - i
            far_on[i] = (jnp.where(hit, k, slot), jnp.where(hit, 1, found))
    out_ref[...] = total
    for i, (slot, found) in enumerate(far_on):
        block = blocks_ref[slot]
        far_on_ref[i] = jnp.where(found == 1, block, jnp.zeros_like(block))


def hand_kernel(own_ref, *refs):
    came_refs, (next_ref, first_ref, give_ref, keep_ref) = refs[:-5], refs[-4:]
    core_0 = first_ref[...] > 0
    total = own_ref[...]
    for came_ref in came_refs:
        total = total + came_ref[...].astype(jnp.float32)
    give_ref[0] = jnp.where(core_0, total[1], total[0])
    keep_ref[...] = jnp.where(core_0, total[0], total[1])
    give_ref[1:] = next_ref[next_ref.shape[0] - 2 :].astype(jnp.float32)


def final_kernel(keep_ref, came_ref, near_ref, far_on_ref, out_ref):
    total = near_ref[...] + keep_ref[...] + came_ref[0]
    for i in range(2):
        total += times_transposed(came_ref[1 + i].astype(jnp.bfloat16), far_on_ref[i])
    out_ref[...] = total.astype(jnp.bfloat16)


def on_device(charges, near_blocks, near_offset, near_count, far_group, far_target, far_v, far_u):
    rhs, size = charges.shape
    groups, owners = lax.axis_size("grp"), lax.axis_size("blk")
    blocks, slots = far_v.shape[1], near_blocks.shape[1]
    rank = far_v.shape[2]
    chips = owners // 2
    lead = groups // 2 + groups // 8
    hops = chips // 2 // REACH
    me = lax.axis_index("blk")
    here, core = lax.shift_right_logical(me, 1), lax.bitwise_and(me, 1)
    far_numbers = jnp.concatenate(
        [
            lax.rem(lead + groups - far_group[0], groups),
            far_slots(far_target[0, :, 0], here, core, chips),
            lax.rem(lead + groups - lax.axis_index("grp"), groups)[None].astype(jnp.int32),
            core[None].astype(jnp.int32),
        ]
    )
    near_place = jnp.where(core == 0, near_offset[0], -near_offset[0]) + slots // 2
    near_place = jnp.where(jnp.arange(slots, dtype=jnp.int32) < near_count, near_place, slots)

    def f32(*shape):
        return jax.ShapeDtypeStruct((*shape, rhs, size), jnp.float32)

    def bf16(*shape):
        return jax.ShapeDtypeStruct((*shape, rhs, size), jnp.bfloat16)

    def around(value, steps):
        pairs = []
        for z in range(chips):
            pairs.append((2 * z, 2 * ((z + steps) % chips)))
            pairs.append((2 * z + 1, 2 * ((z - steps) % chips) + 1))
        return lax.ppermute(value, "blk", pairs)

    def across(value):
        return lax.ppermute(value, "blk", [(i, i ^ 1) for i in range(owners)])

    pooled = lax.all_to_all(
        jnp.broadcast_to(charges[None], (groups, rhs, size)),
        "grp",
        0,
        0,
        axis_index_groups=[[(lead - i) % groups for i in range(groups)]],
    )
    parts, is_first = local_call(
        far_kernel,
        [f32(2 * chips + 1), f32()],
        far_numbers,
        (pooled, far_v[0], far_u[0]),
        4 * blocks * rhs * rank * size,
        "far_parts",
    )

    taken = across(parts[chips:])
    own, mine, over, *sent = local_call(
        chip_kernel,
        [f32(2 * hops), bf16(2), bf16(2)] + [bf16(2 * hops + more) for more in (2, 1, 2)],
        None,
        (is_first, parts, taken),
        rhs * size,
        "chip_sums",
    )

    landed = {step: around(sent[step - 1], step) for step in (3, 2, 1)}
    opposite = lax.ppermute(
        over, "blk", [(2 * z + 1, 2 * ((z - REACH) % chips) + 1) for z in range(chips)]
    )
    keep, *sent = local_call(
        gather_kernel,
        [f32(2)] + [bf16(2)] * (hops - 1),
        None,
        (opposite, landed[3], landed[2], landed[1], own),
        rhs * size,
        "first_step_sums",
    )

    came = [around(sent[hop - 1], hop * REACH) for hop in range(hops - 1, 0, -1)]

    near, far_on = local_call(
        near_kernel,
        [f32(), jax.ShapeDtypeStruct((2, size, size), jnp.bfloat16)],
        near_place,
        (landed[3], landed[2], landed[1], mine, near_blocks[0]),
        2 * slots * rhs * size * size,
        "near_sum",
    )

    give, keep = local_call(
        hand_kernel,
        [f32(3), f32()],
        None,
        (keep, *came, landed[3], landed[1], is_first),
        rhs * size,
        "direction_sum",
    )
    return local_call(
        final_kernel,
        bf16(),
        None,
        (keep, across(give), near, far_on),
        4 * rhs * size * size,
        "potentials",
    )


def solution(mesh):
    placed = (
        P(None, ("grp", "blk")),
        P(("grp", "blk"), None, None, None),
        P(("grp", "blk"), None),
        P(("grp", "blk")),
        P(("grp", "blk"), None),
        P(("grp", "blk"), None, None),
        P(("grp", "blk"), None, None, None),
        P(("grp", "blk"), None, None, None),
    )
    return jax.shard_map(
        on_device, mesh=mesh, in_specs=placed, out_specs=P(None, ("grp", "blk")), check_vma=False
    )
```

profile of v0, /device:TPU:1, one launch (start us, length us, event | category | flops | bytes accessed | tf_op | source)
XLA Modules:
  0.0 86.3 jit_solution(2504664082982330737)
XLA Ops:
  0.0 1.5 %broadcast_in_dim.18 = bf16[16,64,128]{2,1,0:T(8,128)(2,1)} broadcast(bf16[64,128]{1,0:T(8,128)(2,1)} %param.8), dimensions={1,2} | broadcast | bytes 278528 | tf_op jit(solution)/shard_map/broadcast_in_dim | solution.py:178
  1.5 9.6 %all-to-all-start = ((bf16[16,64,128]{2,1,0:T(8,128)(2,1)}), bf16[16,64,128]{2,1,0:T(8,128)(2,1)S(1)}, u32[]{:S(2)}, u32[]{:S(2)}) async-start(bf16[16,64,128]{2,1,0:T(8,128)(2,1)} %broadcast_in_dim.18), calls=%async_computation | async-start | bytes 524288 | tf_op jit(solution)/shard_map/all_to_all | solution.py:177
  11.1 0.7 compare_select_fusion.3
  11.8 0.1 pad_add_fusion.number_ref
  11.9 2.1 %all-to-all-done.pooled_ref = bf16[16,64,128]{2,1,0:T(8,128)(2,1)S(1)} async-done(((bf16[16,64,128]{2,1,0:T(8,128)(2,1)}), bf16[16,64,128]{2,1,0:T(8,128)(2,1)S(1)}, u32[]{:S(2)}, u32[]{:S(2)}) %all-to-all-start) | async-done | bytes 262176 | tf_op jit(solution)/shard_map/all_to_all | solution.py:177
  14.0 1.3 %far_parts.1 = (f32[65,64,128]{2,1,0:T(8,128)S(1)}, f32[64,128]{1,0:T(8,128)S(1)}) custom-call(s32[98]{0:T(128)S(1)} %pad_add_fusion.number_ref, bf16[16,64,128]{2,1,0:T(8,128)(2,1)S(1)} %all-to-all-done.pooled_ref, bf16[48,32,128]{2,1,0:T(8,128)(2,1)S(1)} %bitcast.20, bf16[48,32,128]{2,1,0:T(8,128)(2,1)S(1)} %bitcast.21), custom_call_target="tpu_custom_call" | custom-call | flops 50331648 | bytes 1048576 | tf_op jit(solution)/shard_map/far_parts/pallas_call | solution.py:15
  15.4 14.5 %collective-permute-start = (f32[33,64,128]{2,1,0:T(8,128)S(1)}, f32[33,64,128]{2,1,0:T(8,128)S(1)}, u32[]{:S(2)}, u32[]{:S(2)}) collective-permute-start(f32[33,64,128]{2,1,0:T(8,128)S(1)} %slice.3), channel_id=1, source_target_pairs={{0,1},{1,0},{2,3},{3,2},{4,5},{5,4},{6,7},{7,6},{8,9},{9,8},{10,11... | collective-permute-start | bytes 3244040 | tf_op jit(solution)/shard_map/ppermute | solution.py:175
  29.9 2.3 %collective-permute-done.taken_ref = f32[33,64,128]{2,1,0:T(8,128)S(1)} collective-permute-done((f32[33,64,128]{2,1,0:T(8,128)S(1)}, f32[33,64,128]{2,1,0:T(8,128)S(1)}, u32[]{:S(2)}, u32[]{:S(2)}) %collective-permute-start) | collective-permute-done | bytes 1081376 | tf_op jit(solution)/shard_map/ppermute | solution.py:175
  32.3 0.1 chip_sums.1
  32.4 8.9 %collective-permute-start.2 = (bf16[10,64,128]{2,1,0:T(8,128)(2,1)S(1)}, bf16[10,64,128]{2,1,0:T(8,128)(2,1)S(1)}, u32[]{:S(2)}, u32[]{:S(2)}) collective-permute-start(bf16[10,64,128]{2,1,0:T(8,128)(2,1)S(1)} %get-tuple-element.24), channel_id=1, source_target_pairs={{0,6},{1,59},{2,8},{3,61},{4,10},{5,63},{6,12},{7,1},{8,14},{9,3},... | collective-permute-start | bytes 491528 | tf_op jit(solution)/shard_map/ppermute | solution.py:172
  41.3 2.6 %collective-permute-start.4 = (bf16[10,64,128]{2,1,0:T(8,128)(2,1)S(1)}, bf16[10,64,128]{2,1,0:T(8,128)(2,1)S(1)}, u32[]{:S(2)}, u32[]{:S(2)}) collective-permute-start(bf16[10,64,128]{2,1,0:T(8,128)(2,1)S(1)} %get-tuple-element.26), channel_id=1, source_target_pairs={{0,2},{1,63},{2,4},{3,1},{4,6},{5,3},{6,8},{7,5},{8,10},{9,7},{10,... | collective-permute-start | bytes 491528 | tf_op jit(solution)/shard_map/ppermute | solution.py:172
  43.9 4.3 %collective-permute-start.3 = (bf16[9,64,128]{2,1,0:T(8,128)(2,1)S(1)}, bf16[9,64,128]{2,1,0:T(8,128)(2,1)S(1)}, u32[]{:S(2)}, u32[]{:S(2)}) collective-permute-start(bf16[9,64,128]{2,1,0:T(8,128)(2,1)S(1)} %get-tuple-element.25), channel_id=1, source_target_pairs={{0,4},{1,61},{2,6},{3,63},{4,8},{5,1},{6,10},{7,3},{8,12},{9,5},{1... | collective-permute-start | bytes 442376 | tf_op jit(solution)/shard_map/ppermute | solution.py:172
  48.2 5.2 %collective-permute-start.1 = (bf16[2,64,128]{2,1,0:T(8,128)(2,1)S(1)}, bf16[2,64,128]{2,1,0:T(8,128)(2,1)S(1)}, u32[]{:S(2)}, u32[]{:S(2)}) collective-permute-start(bf16[2,64,128]{2,1,0:T(8,128)(2,1)S(1)} %get-tuple-element.23), channel_id=1, source_target_pairs={{1,57},{3,59},{5,61},{7,63},{9,1},{11,3},{13,5},{15,7},{17,9},{19,... | collective-permute-start | bytes 98312 | tf_op jit(solution)/shard_map/ppermute | solution.py:204
  53.4 4.1 %collective-permute-done.1.refs_0_ = bf16[2,64,128]{2,1,0:T(8,128)(2,1)S(1)} collective-permute-done((bf16[2,64,128]{2,1,0:T(8,128)(2,1)S(1)}, bf16[2,64,128]{2,1,0:T(8,128)(2,1)S(1)}, u32[]{:S(2)}, u32[]{:S(2)}) %collective-permute-start.1) | collective-permute-done | bytes 32800 | tf_op jit(solution)/shard_map/ppermute | solution.py:204
  57.6 8.6 %collective-permute-start.5 = (bf16[2,64,128]{2,1,0:T(8,128)(2,1)S(1)}, bf16[2,64,128]{2,1,0:T(8,128)(2,1)S(1)}, u32[]{:S(2)}, u32[]{:S(2)}) collective-permute-start(bf16[2,64,128]{2,1,0:T(8,128)(2,1)S(1)} %get-tuple-element.29), channel_id=1, source_target_pairs={{0,24},{1,41},{2,26},{3,43},{4,28},{5,45},{6,30},{7,47},{8,32},{9,... | collective-permute-start | bytes 98312 | tf_op jit(solution)/shard_map/ppermute | solution.py:172
  66.3 4.9 %collective-permute-start.6 = (bf16[2,64,128]{2,1,0:T(8,128)(2,1)S(1)}, bf16[2,64,128]{2,1,0:T(8,128)(2,1)S(1)}, u32[]{:S(2)}, u32[]{:S(2)}) collective-permute-start(bf16[2,64,128]{2,1,0:T(8,128)(2,1)S(1)} %get-tuple-element.30), channel_id=1, source_target_pairs={{0,16},{1,49},{2,18},{3,51},{4,20},{5,53},{6,22},{7,55},{8,24},{9,... | collective-permute-start | bytes 98312 | tf_op jit(solution)/shard_map/ppermute | solution.py:172
  71.1 3.3 %collective-permute-start.7 = (bf16[2,64,128]{2,1,0:T(8,128)(2,1)S(1)}, bf16[2,64,128]{2,1,0:T(8,128)(2,1)S(1)}, u32[]{:S(2)}, u32[]{:S(2)}) collective-permute-start(bf16[2,64,128]{2,1,0:T(8,128)(2,1)S(1)} %get-tuple-element.31), channel_id=1, source_target_pairs={{0,8},{1,57},{2,10},{3,59},{4,12},{5,61},{6,14},{7,63},{8,16},{9,1... | collective-permute-start | bytes 98312 | tf_op jit(solution)/shard_map/ppermute | solution.py:172
  75.1 3.1 %collective-permute-done.5.refs_0_ = bf16[2,64,128]{2,1,0:T(8,128)(2,1)S(1)} collective-permute-done((bf16[2,64,128]{2,1,0:T(8,128)(2,1)S(1)}, bf16[2,64,128]{2,1,0:T(8,128)(2,1)S(1)}, u32[]{:S(2)}, u32[]{:S(2)}) %collective-permute-start.5) | collective-permute-done | bytes 32800 | tf_op jit(solution)/shard_map/ppermute | solution.py:172
  78.2 1.5 %collective-permute-done.6.refs_1_ = bf16[2,64,128]{2,1,0:T(8,128)(2,1)S(1)} collective-permute-done((bf16[2,64,128]{2,1,0:T(8,128)(2,1)S(1)}, bf16[2,64,128]{2,1,0:T(8,128)(2,1)S(1)}, u32[]{:S(2)}, u32[]{:S(2)}) %collective-permute-start.6) | collective-permute-done | bytes 32800 | tf_op jit(solution)/shard_map/ppermute | solution.py:172
  79.6 1.5 %collective-permute-done.7.refs_2_ = bf16[2,64,128]{2,1,0:T(8,128)(2,1)S(1)} collective-permute-done((bf16[2,64,128]{2,1,0:T(8,128)(2,1)S(1)}, bf16[2,64,128]{2,1,0:T(8,128)(2,1)S(1)}, u32[]{:S(2)}, u32[]{:S(2)}) %collective-permute-start.7) | collective-permute-done | bytes 32800 | tf_op jit(solution)/shard_map/ppermute | solution.py:172
  81.2 3.4 %collective-permute-start.8 = (f32[3,64,128]{2,1,0:T(8,128)S(1)}, f32[3,64,128]{2,1,0:T(8,128)S(1)}, u32[]{:S(2)}, u32[]{:S(2)}) collective-permute-start(f32[3,64,128]{2,1,0:T(8,128)S(1)} %get-tuple-element.33), channel_id=1, source_target_pairs={{0,1},{1,0},{2,3},{3,2},{4,5},{5,4},{6,7},{7,6},{8,9},{9,8},{10,11... | collective-permute-start | bytes 294920 | tf_op jit(solution)/shard_map/ppermute | solution.py:175
  84.6 0.8 near_sum.1
  85.4 0.1 collective-permute-done.8.came_ref
  85.5 0.8 potentials.1
  (15 shorter events, 0.2 us)
Async XLA Ops:
  0.0 14.0 %copy-start.1 = (bf16[1,48,32,128]{3,2,1,0:T(8,128)(2,1)S(1)}, bf16[1,48,32,128]{3,2,1,0:T(8,128)(2,1)}, u32[]{:S(2)}) copy-start(bf16[1,48,32,128]{3,2,1,0:T(8,128)(2,1)} %param.15) | copy-start | bytes 1179652
  0.0 14.0 %copy-start = (bf16[1,48,32,128]{3,2,1,0:T(8,128)(2,1)S(1)}, bf16[1,48,32,128]{3,2,1,0:T(8,128)(2,1)}, u32[]{:S(2)}) copy-start(bf16[1,48,32,128]{3,2,1,0:T(8,128)(2,1)} %param.14) | copy-start | bytes 1179652
  1.5 12.5 %all-to-all-start = ((bf16[16,64,128]{2,1,0:T(8,128)(2,1)}), bf16[16,64,128]{2,1,0:T(8,128)(2,1)S(1)}, u32[]{:S(2)}, u32[]{:S(2)}) async-start(bf16[16,64,128]{2,1,0:T(8,128)(2,1)} %broadcast_in_dim.18), calls=%async_computation | async-start | bytes 524288 | tf_op jit(solution)/shard_map/all_to_all | solution.py:177
  15.4 16.9 %collective-permute-start = (f32[33,64,128]{2,1,0:T(8,128)S(1)}, f32[33,64,128]{2,1,0:T(8,128)S(1)}, u32[]{:S(2)}, u32[]{:S(2)}) collective-permute-start(f32[33,64,128]{2,1,0:T(8,128)S(1)} %slice.3), channel_id=1, source_target_pairs={{0,1},{1,0},{2,3},{3,2},{4,5},{5,4},{6,7},{7,6},{8,9},{9,8},{10,11... | collective-permute-start | bytes 3244040 | tf_op jit(solution)/shard_map/ppermute | solution.py:175
  32.4 52.2 %copy-start.3 = (s32[1,7]{1,0:T(1,128)S(1)}, s32[1,7]{1,0:T(1,128)}, u32[]{:S(2)}) copy-start(s32[1,7]{1,0:T(1,128)} %param.10) | copy-start | bytes 88
  32.4 52.2 %copy-start.2 = (bf16[1,7,128,128]{3,2,1,0:T(8,128)(2,1)S(1)}, bf16[1,7,128,128]{3,2,1,0:T(8,128)(2,1)}, u32[]{:S(2)}) copy-start(bf16[1,7,128,128]{3,2,1,0:T(8,128)(2,1)} %param.9) | copy-start | bytes 688132
  32.4 25.2 %collective-permute-start.2 = (bf16[10,64,128]{2,1,0:T(8,128)(2,1)S(1)}, bf16[10,64,128]{2,1,0:T(8,128)(2,1)S(1)}, u32[]{:S(2)}, u32[]{:S(2)}) collective-permute-start(bf16[10,64,128]{2,1,0:T(8,128)(2,1)S(1)} %get-tuple-element.24), channel_id=1, source_target_pairs={{0,6},{1,59},{2,8},{3,61},{4,10},{5,63},{6,12},{7,1},{8,14},{9,3},... | collective-permute-start | bytes 491528 | tf_op jit(solution)/shard_map/ppermute | solution.py:172
  41.3 16.3 %collective-permute-start.4 = (bf16[10,64,128]{2,1,0:T(8,128)(2,1)S(1)}, bf16[10,64,128]{2,1,0:T(8,128)(2,1)S(1)}, u32[]{:S(2)}, u32[]{:S(2)}) collective-permute-start(bf16[10,64,128]{2,1,0:T(8,128)(2,1)S(1)} %get-tuple-element.26), channel_id=1, source_target_pairs={{0,2},{1,63},{2,4},{3,1},{4,6},{5,3},{6,8},{7,5},{8,10},{9,7},{10,... | collective-permute-start | bytes 491528 | tf_op jit(solution)/shard_map/ppermute | solution.py:172
  43.9 13.6 %collective-permute-start.3 = (bf16[9,64,128]{2,1,0:T(8,128)(2,1)S(1)}, bf16[9,64,128]{2,1,0:T(8,128)(2,1)S(1)}, u32[]{:S(2)}, u32[]{:S(2)}) collective-permute-start(bf16[9,64,128]{2,1,0:T(8,128)(2,1)S(1)} %get-tuple-element.25), channel_id=1, source_target_pairs={{0,4},{1,61},{2,6},{3,63},{4,8},{5,1},{6,10},{7,3},{8,12},{9,5},{1... | collective-permute-start | bytes 442376 | tf_op jit(solution)/shard_map/ppermute | solution.py:172
  48.2 9.3 %collective-permute-start.1 = (bf16[2,64,128]{2,1,0:T(8,128)(2,1)S(1)}, bf16[2,64,128]{2,1,0:T(8,128)(2,1)S(1)}, u32[]{:S(2)}, u32[]{:S(2)}) collective-permute-start(bf16[2,64,128]{2,1,0:T(8,128)(2,1)S(1)} %get-tuple-element.23), channel_id=1, source_target_pairs={{1,57},{3,59},{5,61},{7,63},{9,1},{11,3},{13,5},{15,7},{17,9},{19,... | collective-permute-start | bytes 98312 | tf_op jit(solution)/shard_map/ppermute | solution.py:204
  57.6 20.6 %collective-permute-start.5 = (bf16[2,64,128]{2,1,0:T(8,128)(2,1)S(1)}, bf16[2,64,128]{2,1,0:T(8,128)(2,1)S(1)}, u32[]{:S(2)}, u32[]{:S(2)}) collective-permute-start(bf16[2,64,128]{2,1,0:T(8,128)(2,1)S(1)} %get-tuple-element.29), channel_id=1, source_target_pairs={{0,24},{1,41},{2,26},{3,43},{4,28},{5,45},{6,30},{7,47},{8,32},{9,... | collective-permute-start | bytes 98312 | tf_op jit(solution)/shard_map/ppermute | solution.py:172
  66.3 13.4 %collective-permute-start.6 = (bf16[2,64,128]{2,1,0:T(8,128)(2,1)S(1)}, bf16[2,64,128]{2,1,0:T(8,128)(2,1)S(1)}, u32[]{:S(2)}, u32[]{:S(2)}) collective-permute-start(bf16[2,64,128]{2,1,0:T(8,128)(2,1)S(1)} %get-tuple-element.30), channel_id=1, source_target_pairs={{0,16},{1,49},{2,18},{3,51},{4,20},{5,53},{6,22},{7,55},{8,24},{9,... | collective-permute-start | bytes 98312 | tf_op jit(solution)/shard_map/ppermute | solution.py:172
  71.1 10.0 %collective-permute-start.7 = (bf16[2,64,128]{2,1,0:T(8,128)(2,1)S(1)}, bf16[2,64,128]{2,1,0:T(8,128)(2,1)S(1)}, u32[]{:S(2)}, u32[]{:S(2)}) collective-permute-start(bf16[2,64,128]{2,1,0:T(8,128)(2,1)S(1)} %get-tuple-element.31), channel_id=1, source_target_pairs={{0,8},{1,57},{2,10},{3,59},{4,12},{5,61},{6,14},{7,63},{8,16},{9,1... | collective-permute-start | bytes 98312 | tf_op jit(solution)/shard_map/ppermute | solution.py:172
  81.2 4.4 %collective-permute-start.8 = (f32[3,64,128]{2,1,0:T(8,128)S(1)}, f32[3,64,128]{2,1,0:T(8,128)S(1)}, u32[]{:S(2)}, u32[]{:S(2)}) collective-permute-start(f32[3,64,128]{2,1,0:T(8,128)S(1)} %get-tuple-element.33), channel_id=1, source_target_pairs={{0,1},{1,0},{2,3},{3,2},{4,5},{5,4},{6,7},{7,6},{8,9},{9,8},{10,11... | collective-permute-start | bytes 294920 | tf_op jit(solution)/shard_map/ppermute | solution.py:175
where the time goes:
time: 86.8 us; the launch traced here: 86.3 us
  starting transfers between devices  65.3 us (75%)
  waiting for transfers between devices  14.7 us (17%)
  Pallas kernels  3.04 us (4%)
  local copies, waits for them, and re-layouts  1.63 us (2%)
    ppermute x6, starting transfers between devices, around(): return lax.ppermute(value, 'blk', pairs)  32.6 us
    ppermute x2, starting transfers between devices, across(): return lax.ppermute(value, 'blk', [(i, i ^ 1) for i in range(owners)])  18 us
    all_to_all x1, starting transfers between devices, on_device(): lax.all_to_all(jnp.broadcast_to(charges[None], (groups, rhs, size)), 'grp...  9.58 us
    ppermute x6, waiting for transfers between devices, around(): return lax.ppermute(value, 'blk', pairs)  6.07 us
    ppermute x1, starting transfers between devices, on_device(): lax.ppermute(over, 'blk', [(2 * z + 1, 2 * ((z - REACH) % chips) + 1) for...  5.18 us
    ppermute x1, waiting for transfers between devices, on_device(): lax.ppermute(over, 'blk', [(2 * z + 1, 2 * ((z - REACH) % chips) + 1) for...  4.13 us
    pallas_call x6, Pallas kernels, local_call(): pl.pallas_call(kernel, out_shape=outs, in_specs=[pl.BlockSpec(memory_spac...  3.04 us
    ppermute x2, waiting for transfers between devices, across(): return lax.ppermute(value, 'blk', [(i, i ^ 1) for i in range(owners)])  2.41 us
  transfers between devices with their start and end apart: 10, of which 7 were waited for; matrix products, arithmetic and copies ran while one was open for 1% of the time, Pallas kernels for 1%

commit v1 on v0

--- a/solution.py
+++ b/solution.py
@@ -40,10 +40,13 @@
     return slot + lax.bitwise_xor(behind, core) * chips
 
 
-def far_kernel(number_ref, pooled_ref, v_ref, u_ref, out_ref, first_ref):
+def far_kernel(given_ref, pooled_ref, v_ref, u_ref, out_ref, first_ref, number_ref, done):
     blocks, last = v_ref.shape[0], out_ref.shape[0] - 1
+    numbers = pltpu.make_async_copy(given_ref, number_ref, done)
+    numbers.start()
     for slot in range(last):
         out_ref[slot] = jnp.zeros(out_ref.shape[1:], jnp.float32)
+    numbers.wait()
     first_ref[...] = jnp.where(
         number_ref[2 * blocks + 1] == 0,
         jnp.ones(first_ref.shape, jnp.float32),
@@ -181,14 +184,24 @@
         0,
         axis_index_groups=[[(lead - i) % groups for i in range(groups)]],
     )
-    parts, is_first = local_call(
+    arrays = (far_numbers, pooled, far_v[0], far_u[0])
+    parts, is_first = pl.pallas_call(
         far_kernel,
-        [f32(2 * chips + 1), f32()],
-        far_numbers,
-        (pooled, far_v[0], far_u[0]),
-        4 * blocks * rhs * rank * size,
-        "far_parts",
-    )
+        out_shape=[f32(2 * chips + 1), f32()],
+        in_specs=[pl.BlockSpec(memory_space=pl.ANY)] + [pl.BlockSpec(memory_space=VMEM)] * 3,
+        out_specs=[pl.BlockSpec(memory_space=VMEM)] * 2,
+        scratch_shapes=[
+            pltpu.SMEM(far_numbers.shape, far_numbers.dtype),
+            pltpu.SemaphoreType.DMA(()),
+        ],
+        compiler_params=pltpu.CompilerParams(vmem_limit_bytes=24 << 20),
+        cost_estimate=pl.CostEstimate(
+            flops=4 * blocks * rhs * rank * size,
+            bytes_accessed=sum(a.nbytes for a in arrays),
+            transcendentals=0,
+        ),
+        name="far_parts",
+    )(*arrays)
 
     taken = across(parts[chips:])
     own, mine, over, *sent = local_call(

time: 86.8 us -> 86.9 us (level)
    pallas_call x0 -> x1, Pallas kernels: none -> 1.32 us  [on_device(): pl.pallas_call(far_kernel, out_shape=[f32(2 * chips + 1), f32()], in_spec...]
    pallas_call x6 -> x5, Pallas kernels: 3.04 us -> 1.74 us  [local_call(): pl.pallas_call(kernel, out_shape=outs, in_specs=[pl.BlockSpec(memory_spac...]
where the time goes in v1:
time: 86.9 us; the launch traced here: 86.3 us
  starting transfers between devices  65.3 us (75%)
  waiting for transfers between devices  14.7 us (17%)
  Pallas kernels  3.06 us (4%)
  local copies, waits for them, and re-layouts  1.63 us (2%)
    ppermute x6, starting transfers between devices, around(): return lax.ppermute(value, 'blk', pairs)  32.6 us
    ppermute x2, starting transfers between devices, across(): return lax.ppermute(value, 'blk', [(i, i ^ 1) for i in range(owners)])  18 us
    all_to_all x1, starting transfers between devices, on_device(): lax.all_to_all(jnp.broadcast_to(charges[None], (groups, rhs, size)), 'grp...  9.58 us
    ppermute x6, waiting for transfers between devices, around(): return lax.ppermute(value, 'blk', pairs)  6.07 us
    ppermute x1, starting transfers between devices, on_device(): lax.ppermute(over, 'blk', [(2 * z + 1, 2 * ((z - REACH) % chips) + 1) for...  5.18 us
    ppermute x1, waiting for transfers between devices, on_device(): lax.ppermute(over, 'blk', [(2 * z + 1, 2 * ((z - REACH) % chips) + 1) for...  4.13 us
    ppermute x2, waiting for transfers between devices, across(): return lax.ppermute(value, 'blk', [(i, i ^ 1) for i in range(owners)])  2.41 us
    all_to_all x1, waiting for transfers between devices, on_device(): lax.all_to_all(jnp.broadcast_to(charges[None], (groups, rhs, size)), 'grp...  2.11 us
  transfers between devices with their start and end apart: 10, of which 7 were waited for; matrix products, arithmetic and copies ran while one was open for 1% of the time, Pallas kernels for 1%

profile of v1, /device:TPU:1, one launch (start us, length us, event | category | flops | bytes accessed | tf_op | source)
XLA Modules:
  0.0 86.3 jit_solution(257343591905792912)
XLA Ops:
  0.0 1.5 %broadcast_in_dim.18 = bf16[16,64,128]{2,1,0:T(8,128)(2,1)} broadcast(bf16[64,128]{1,0:T(8,128)(2,1)} %param.8), dimensions={1,2} | broadcast | bytes 278528 | tf_op jit(solution)/shard_map/broadcast_in_dim | solution.py:181
  1.5 9.6 %all-to-all-start = ((bf16[16,64,128]{2,1,0:T(8,128)(2,1)}), bf16[16,64,128]{2,1,0:T(8,128)(2,1)S(1)}, u32[]{:S(2)}, u32[]{:S(2)}) async-start(bf16[16,64,128]{2,1,0:T(8,128)(2,1)} %broadcast_in_dim.18), calls=%async_computation | async-start | bytes 524288 | tf_op jit(solution)/shard_map/all_to_all | solution.py:180
  11.1 0.7 compare_select_fusion.3
  11.8 0.1 pad_add_fusion.given_ref
  11.9 2.1 %all-to-all-done.pooled_ref = bf16[16,64,128]{2,1,0:T(8,128)(2,1)S(1)} async-done(((bf16[16,64,128]{2,1,0:T(8,128)(2,1)}), bf16[16,64,128]{2,1,0:T(8,128)(2,1)S(1)}, u32[]{:S(2)}, u32[]{:S(2)}) %all-to-all-start) | async-done | bytes 262176 | tf_op jit(solution)/shard_map/all_to_all | solution.py:180
  14.0 1.3 %far_parts.1 = (f32[65,64,128]{2,1,0:T(8,128)S(1)}, f32[64,128]{1,0:T(8,128)S(1)}) custom-call(s32[98]{0:T(128)S(1)} %pad_add_fusion.given_ref, bf16[16,64,128]{2,1,0:T(8,128)(2,1)S(1)} %all-to-all-done.pooled_ref, bf16[48,32,128]{2,1,0:T(8,128)(2,1)S(1)} %bitcast.20, bf16[48,32,128]{2,1,0:T(8,128)(2,1)S(1)} %bitcast.21), custom_call_target="tpu_custom_call" | custom-call | flops 50331648 | bytes 1048968 | tf_op jit(solution)/shard_map/far_parts/pallas_call | solution.py:188
  15.4 14.5 %collective-permute-start = (f32[33,64,128]{2,1,0:T(8,128)S(1)}, f32[33,64,128]{2,1,0:T(8,128)S(1)}, u32[]{:S(2)}, u32[]{:S(2)}) collective-permute-start(f32[33,64,128]{2,1,0:T(8,128)S(1)} %slice.3), channel_id=1, source_target_pairs={{0,1},{1,0},{2,3},{3,2},{4,5},{5,4},{6,7},{7,6},{8,9},{9,8},{10,11... | collective-permute-start | bytes 3244040 | tf_op jit(solution)/shard_map/ppermute | solution.py:178
  30.0 2.3 %collective-permute-done.taken_ref = f32[33,64,128]{2,1,0:T(8,128)S(1)} collective-permute-done((f32[33,64,128]{2,1,0:T(8,128)S(1)}, f32[33,64,128]{2,1,0:T(8,128)S(1)}, u32[]{:S(2)}, u32[]{:S(2)}) %collective-permute-start) | collective-permute-done | bytes 1081376 | tf_op jit(solution)/shard_map/ppermute | solution.py:178
  32.3 0.1 chip_sums.1
  32.4 8.9 %collective-permute-start.2 = (bf16[10,64,128]{2,1,0:T(8,128)(2,1)S(1)}, bf16[10,64,128]{2,1,0:T(8,128)(2,1)S(1)}, u32[]{:S(2)}, u32[]{:S(2)}) collective-permute-start(bf16[10,64,128]{2,1,0:T(8,128)(2,1)S(1)} %get-tuple-element.24), channel_id=1, source_target_pairs={{0,6},{1,59},{2,8},{3,61},{4,10},{5,63},{6,12},{7,1},{8,14},{9,3},... | collective-permute-start | bytes 491528 | tf_op jit(solution)/shard_map/ppermute | solution.py:175
  41.3 2.6 %collective-permute-start.4 = (bf16[10,64,128]{2,1,0:T(8,128)(2,1)S(1)}, bf16[10,64,128]{2,1,0:T(8,128)(2,1)S(1)}, u32[]{:S(2)}, u32[]{:S(2)}) collective-permute-start(bf16[10,64,128]{2,1,0:T(8,128)(2,1)S(1)} %get-tuple-element.26), channel_id=1, source_target_pairs={{0,2},{1,63},{2,4},{3,1},{4,6},{5,3},{6,8},{7,5},{8,10},{9,7},{10,... | collective-permute-start | bytes 491528 | tf_op jit(solution)/shard_map/ppermute | solution.py:175
  43.9 4.3 %collective-permute-start.3 = (bf16[9,64,128]{2,1,0:T(8,128)(2,1)S(1)}, bf16[9,64,128]{2,1,0:T(8,128)(2,1)S(1)}, u32[]{:S(2)}, u32[]{:S(2)}) collective-permute-start(bf16[9,64,128]{2,1,0:T(8,128)(2,1)S(1)} %get-tuple-element.25), channel_id=1, source_target_pairs={{0,4},{1,61},{2,6},{3,63},{4,8},{5,1},{6,10},{7,3},{8,12},{9,5},{1... | collective-permute-start | bytes 442376 | tf_op jit(solution)/shard_map/ppermute | solution.py:175
  48.2 5.2 %collective-permute-start.1 = (bf16[2,64,128]{2,1,0:T(8,128)(2,1)S(1)}, bf16[2,64,128]{2,1,0:T(8,128)(2,1)S(1)}, u32[]{:S(2)}, u32[]{:S(2)}) collective-permute-start(bf16[2,64,128]{2,1,0:T(8,128)(2,1)S(1)} %get-tuple-element.23), channel_id=1, source_target_pairs={{1,57},{3,59},{5,61},{7,63},{9,1},{11,3},{13,5},{15,7},{17,9},{19,... | collective-permute-start | bytes 98312 | tf_op jit(solution)/shard_map/ppermute | solution.py:217
  53.4 4.1 %collective-permute-done.1.refs_0_ = bf16[2,64,128]{2,1,0:T(8,128)(2,1)S(1)} collective-permute-done((bf16[2,64,128]{2,1,0:T(8,128)(2,1)S(1)}, bf16[2,64,128]{2,1,0:T(8,128)(2,1)S(1)}, u32[]{:S(2)}, u32[]{:S(2)}) %collective-permute-start.1) | collective-permute-done | bytes 32800 | tf_op jit(solution)/shard_map/ppermute | solution.py:217
  57.6 8.6 %collective-permute-start.5 = (bf16[2,64,128]{2,1,0:T(8,128)(2,1)S(1)}, bf16[2,64,128]{2,1,0:T(8,128)(2,1)S(1)}, u32[]{:S(2)}, u32[]{:S(2)}) collective-permute-start(bf16[2,64,128]{2,1,0:T(8,128)(2,1)S(1)} %get-tuple-element.29), channel_id=1, source_target_pairs={{0,24},{1,41},{2,26},{3,43},{4,28},{5,45},{6,30},{7,47},{8,32},{9,... | collective-permute-start | bytes 98312 | tf_op jit(solution)/shard_map/ppermute | solution.py:175
  66.3 4.9 %collective-permute-start.6 = (bf16[2,64,128]{2,1,0:T(8,128)(2,1)S(1)}, bf16[2,64,128]{2,1,0:T(8,128)(2,1)S(1)}, u32[]{:S(2)}, u32[]{:S(2)}) collective-permute-start(bf16[2,64,128]{2,1,0:T(8,128)(2,1)S(1)} %get-tuple-element.30), channel_id=1, source_target_pairs={{0,16},{1,49},{2,18},{3,51},{4,20},{5,53},{6,22},{7,55},{8,24},{9,... | collective-permute-start | bytes 98312 | tf_op jit(solution)/shard_map/ppermute | solution.py:175
  71.2 3.3 %collective-permute-start.7 = (bf16[2,64,128]{2,1,0:T(8,128)(2,1)S(1)}, bf16[2,64,128]{2,1,0:T(8,128)(2,1)S(1)}, u32[]{:S(2)}, u32[]{:S(2)}) collective-permute-start(bf16[2,64,128]{2,1,0:T(8,128)(2,1)S(1)} %get-tuple-element.31), channel_id=1, source_target_pairs={{0,8},{1,57},{2,10},{3,59},{4,12},{5,61},{6,14},{7,63},{8,16},{9,1... | collective-permute-start | bytes 98312 | tf_op jit(solution)/shard_map/ppermute | solution.py:175
  75.1 3.1 %collective-permute-done.5.refs_0_ = bf16[2,64,128]{2,1,0:T(8,128)(2,1)S(1)} collective-permute-done((bf16[2,64,128]{2,1,0:T(8,128)(2,1)S(1)}, bf16[2,64,128]{2,1,0:T(8,128)(2,1)S(1)}, u32[]{:S(2)}, u32[]{:S(2)}) %collective-permute-start.5) | collective-permute-done | bytes 32800 | tf_op jit(solution)/shard_map/ppermute | solution.py:175
  78.2 1.5 %collective-permute-done.6.refs_1_ = bf16[2,64,128]{2,1,0:T(8,128)(2,1)S(1)} collective-permute-done((bf16[2,64,128]{2,1,0:T(8,128)(2,1)S(1)}, bf16[2,64,128]{2,1,0:T(8,128)(2,1)S(1)}, u32[]{:S(2)}, u32[]{:S(2)}) %collective-permute-start.6) | collective-permute-done | bytes 32800 | tf_op jit(solution)/shard_map/ppermute | solution.py:175
  79.7 1.5 %collective-permute-done.7.refs_2_ = bf16[2,64,128]{2,1,0:T(8,128)(2,1)S(1)} collective-permute-done((bf16[2,64,128]{2,1,0:T(8,128)(2,1)S(1)}, bf16[2,64,128]{2,1,0:T(8,128)(2,1)S(1)}, u32[]{:S(2)}, u32[]{:S(2)}) %collective-permute-start.7) | collective-permute-done | bytes 32800 | tf_op jit(solution)/shard_map/ppermute | solution.py:175
  81.2 3.4 %collective-permute-start.8 = (f32[3,64,128]{2,1,0:T(8,128)S(1)}, f32[3,64,128]{2,1,0:T(8,128)S(1)}, u32[]{:S(2)}, u32[]{:S(2)}) collective-permute-start(f32[3,64,128]{2,1,0:T(8,128)S(1)} %get-tuple-element.33), channel_id=1, source_target_pairs={{0,1},{1,0},{2,3},{3,2},{4,5},{5,4},{6,7},{7,6},{8,9},{9,8},{10,11... | collective-permute-start | bytes 294920 | tf_op jit(solution)/shard_map/ppermute | solution.py:178
  84.7 0.8 near_sum.1
  85.4 0.1 collective-permute-done.8.came_ref
  85.5 0.8 potentials.1
  (15 shorter events, 0.2 us)
Async XLA Ops:
  0.0 14.0 %copy-start.1 = (bf16[1,48,32,128]{3,2,1,0:T(8,128)(2,1)S(1)}, bf16[1,48,32,128]{3,2,1,0:T(8,128)(2,1)}, u32[]{:S(2)}) copy-start(bf16[1,48,32,128]{3,2,1,0:T(8,128)(2,1)} %param.15) | copy-start | bytes 1179652
  0.0 14.0 %copy-start = (bf16[1,48,32,128]{3,2,1,0:T(8,128)(2,1)S(1)}, bf16[1,48,32,128]{3,2,1,0:T(8,128)(2,1)}, u32[]{:S(2)}) copy-start(bf16[1,48,32,128]{3,2,1,0:T(8,128)(2,1)} %param.14) | copy-start | bytes 1179652
  1.5 12.5 %all-to-all-start = ((bf16[16,64,128]{2,1,0:T(8,128)(2,1)}), bf16[16,64,128]{2,1,0:T(8,128)(2,1)S(1)}, u32[]{:S(2)}, u32[]{:S(2)}) async-start(bf16[16,64,128]{2,1,0:T(8,128)(2,1)} %broadcast_in_dim.18), calls=%async_computation | async-start | bytes 524288 | tf_op jit(solution)/shard_map/all_to_all | solution.py:180
  15.4 16.9 %collective-permute-start = (f32[33,64,128]{2,1,0:T(8,128)S(1)}, f32[33,64,128]{2,1,0:T(8,128)S(1)}, u32[]{:S(2)}, u32[]{:S(2)}) collective-permute-start(f32[33,64,128]{2,1,0:T(8,128)S(1)} %slice.3), channel_id=1, source_target_pairs={{0,1},{1,0},{2,3},{3,2},{4,5},{5,4},{6,7},{7,6},{8,9},{9,8},{10,11... | collective-permute-start | bytes 3244040 | tf_op jit(solution)/shard_map/ppermute | solution.py:178
  32.4 52.2 %copy-start.3 = (s32[1,7]{1,0:T(1,128)S(1)}, s32[1,7]{1,0:T(1,128)}, u32[]{:S(2)}) copy-start(s32[1,7]{1,0:T(1,128)} %param.10) | copy-start | bytes 88
  32.4 52.2 %copy-start.2 = (bf16[1,7,128,128]{3,2,1,0:T(8,128)(2,1)S(1)}, bf16[1,7,128,128]{3,2,1,0:T(8,128)(2,1)}, u32[]{:S(2)}) copy-start(bf16[1,7,128,128]{3,2,1,0:T(8,128)(2,1)} %param.9) | copy-start | bytes 688132
  32.4 25.2 %collective-permute-start.2 = (bf16[10,64,128]{2,1,0:T(8,128)(2,1)S(1)}, bf16[10,64,128]{2,1,0:T(8,128)(2,1)S(1)}, u32[]{:S(2)}, u32[]{:S(2)}) collective-permute-start(bf16[10,64,128]{2,1,0:T(8,128)(2,1)S(1)} %get-tuple-element.24), channel_id=1, source_target_pairs={{0,6},{1,59},{2,8},{3,61},{4,10},{5,63},{6,12},{7,1},{8,14},{9,3},... | collective-permute-start | bytes 491528 | tf_op jit(solution)/shard_map/ppermute | solution.py:175
  41.3 16.3 %collective-permute-start.4 = (bf16[10,64,128]{2,1,0:T(8,128)(2,1)S(1)}, bf16[10,64,128]{2,1,0:T(8,128)(2,1)S(1)}, u32[]{:S(2)}, u32[]{:S(2)}) collective-permute-start(bf16[10,64,128]{2,1,0:T(8,128)(2,1)S(1)} %get-tuple-element.26), channel_id=1, source_target_pairs={{0,2},{1,63},{2,4},{3,1},{4,6},{5,3},{6,8},{7,5},{8,10},{9,7},{10,... | collective-permute-start | bytes 491528 | tf_op jit(solution)/shard_map/ppermute | solution.py:175
  43.9 13.6 %collective-permute-start.3 = (bf16[9,64,128]{2,1,0:T(8,128)(2,1)S(1)}, bf16[9,64,128]{2,1,0:T(8,128)(2,1)S(1)}, u32[]{:S(2)}, u32[]{:S(2)}) collective-permute-start(bf16[9,64,128]{2,1,0:T(8,128)(2,1)S(1)} %get-tuple-element.25), channel_id=1, source_target_pairs={{0,4},{1,61},{2,6},{3,63},{4,8},{5,1},{6,10},{7,3},{8,12},{9,5},{1... | collective-permute-start | bytes 442376 | tf_op jit(solution)/shard_map/ppermute | solution.py:175
  48.2 9.3 %collective-permute-start.1 = (bf16[2,64,128]{2,1,0:T(8,128)(2,1)S(1)}, bf16[2,64,128]{2,1,0:T(8,128)(2,1)S(1)}, u32[]{:S(2)}, u32[]{:S(2)}) collective-permute-start(bf16[2,64,128]{2,1,0:T(8,128)(2,1)S(1)} %get-tuple-element.23), channel_id=1, source_target_pairs={{1,57},{3,59},{5,61},{7,63},{9,1},{11,3},{13,5},{15,7},{17,9},{19,... | collective-permute-start | bytes 98312 | tf_op jit(solution)/shard_map/ppermute | solution.py:217
  57.6 20.6 %collective-permute-start.5 = (bf16[2,64,128]{2,1,0:T(8,128)(2,1)S(1)}, bf16[2,64,128]{2,1,0:T(8,128)(2,1)S(1)}, u32[]{:S(2)}, u32[]{:S(2)}) collective-permute-start(bf16[2,64,128]{2,1,0:T(8,128)(2,1)S(1)} %get-tuple-element.29), channel_id=1, source_target_pairs={{0,24},{1,41},{2,26},{3,43},{4,28},{5,45},{6,30},{7,47},{8,32},{9,... | collective-permute-start | bytes 98312 | tf_op jit(solution)/shard_map/ppermute | solution.py:175
  66.3 13.4 %collective-permute-start.6 = (bf16[2,64,128]{2,1,0:T(8,128)(2,1)S(1)}, bf16[2,64,128]{2,1,0:T(8,128)(2,1)S(1)}, u32[]{:S(2)}, u32[]{:S(2)}) collective-permute-start(bf16[2,64,128]{2,1,0:T(8,128)(2,1)S(1)} %get-tuple-element.30), channel_id=1, source_target_pairs={{0,16},{1,49},{2,18},{3,51},{4,20},{5,53},{6,22},{7,55},{8,24},{9,... | collective-permute-start | bytes 98312 | tf_op jit(solution)/shard_map/ppermute | solution.py:175
  71.2 10.0 %collective-permute-start.7 = (bf16[2,64,128]{2,1,0:T(8,128)(2,1)S(1)}, bf16[2,64,128]{2,1,0:T(8,128)(2,1)S(1)}, u32[]{:S(2)}, u32[]{:S(2)}) collective-permute-start(bf16[2,64,128]{2,1,0:T(8,128)(2,1)S(1)} %get-tuple-element.31), channel_id=1, source_target_pairs={{0,8},{1,57},{2,10},{3,59},{4,12},{5,61},{6,14},{7,63},{8,16},{9,1... | collective-permute-start | bytes 98312 | tf_op jit(solution)/shard_map/ppermute | solution.py:175
  81.2 4.4 %collective-permute-start.8 = (f32[3,64,128]{2,1,0:T(8,128)S(1)}, f32[3,64,128]{2,1,0:T(8,128)S(1)}, u32[]{:S(2)}, u32[]{:S(2)}) collective-permute-start(f32[3,64,128]{2,1,0:T(8,128)S(1)} %get-tuple-element.33), channel_id=1, source_target_pairs={{0,1},{1,0},{2,3},{3,2},{4,5},{5,4},{6,7},{7,6},{8,9},{9,8},{10,11... | collective-permute-start | bytes 294920 | tf_op jit(solution)/shard_map/ppermute | solution.py:178
